TPU v7x, 32 devices: a whole 2x2x4 slice. The times are simulated.
32 devices in a mesh: sa: 4 (over z), sb: 4 (over x, core), rep: 2 (over y).
Axes of the slice: x: 2, y: 2, z: 4, core: 2. Of those that a mesh axis runs over, the one named last changes fastest.
Arguments:
- queries: bfloat16 [2, 64, 64, 12288], P('rep', ('sa', 'sb')), may hold values from -90.93267 to 90.93267
- grad_out: bfloat16 [2, 64, 64, 8192], P('rep', ('sa', 'sb')), may hold values from -6 to 6
- cache_codes: bfloat16 [2, 320, 16, 576], P('rep', ('sa', 'sb')), may hold values from -4.1 to 4.1
- cache_exponents: int32 [2, 320, 16, 4], P('rep', ('sa', 'sb')), may hold values from -1 to 1
- page_table: int32 [2, 64, 5], P('rep'), may hold values from 0 to 319, as said below
- offsets: int32 [2, 64], P('rep'), may hold values from 8 to 16, as said below
- key_up: bfloat16 [64, 512, 128], P(('sa', 'sb')), may hold values from -0.25 to 0.25
- value_up: bfloat16 [64, 512, 128], P(('sa', 'sb')), may hold values from -0.25 to 0.25
Outputs:
- grad_queries: bfloat16 [2, 64, 64, 12288], P('rep', ('sa', 'sb'))
- grad_cache: float32 [2, 320, 16, 576], P('rep', ('sa', 'sb'))
- grad_key_up: float32 [64, 512, 128], P(('sa', 'sb'))
- grad_value_up: float32 [64, 512, 128], P(('sa', 'sb'))
Inputs may be any that keep to these rules, and one draw needn't show every extreme that they name: `page_table`: the rows of the sequences of one replica together name each of that replica's 320 pool pages exactly once. Query i of sequence s of replica r stands at key position offsets[r, s] + i.
All inputs are finite; a program needn't handle non-finite values.
Results may differ from a plain program's by a relative error of at most 0.015.
Values may be sent and summed in bfloat16 or wider, within the bound.
A program may use at most 128 MiB of HBM per device.

v0:
```python
import jax
import jax.numpy as jnp
from jax import lax
from jax.sharding import PartitionSpec as P

RANK = 512
ROPE = 64
NOPE = 128
VDIM = 128
PAGE = 16


def dequantize(stored, exponents):
    block_size = RANK // exponents.shape[-1]
    factor = jnp.repeat(jnp.exp2(exponents.astype(jnp.float32)), block_size, axis=-1)
    latent = (stored[..., :RANK].astype(jnp.float32) * factor).astype(jnp.bfloat16)
    return jnp.concatenate([latent, stored[..., RANK:]], axis=-1)


def sequence_grads(query_rows, grad_rows, seq_keys, start, key_up, value_up):
    head_count = key_up.shape[0]
    row_count = query_rows.shape[0]
    key_count = seq_keys.shape[0]
    softmax_scale = (NOPE + ROPE) ** (-0.5)
    split_rows = query_rows.reshape(row_count, head_count, NOPE + ROPE)
    query_nope = split_rows[:, :, :NOPE]
    query_rope = jnp.transpose(split_rows[:, :, NOPE:], (1, 0, 2))
    latent = seq_keys[:, :RANK]
    query_lat = jnp.einsum(
        "qhd,hrd->hqr", query_nope, key_up, preferred_element_type=jnp.float32
    ).astype(jnp.bfloat16)
    query_full = jnp.concatenate([query_lat, query_rope], axis=-1)
    scores = (
        jnp.einsum("hqc,kc->hqk", query_full, seq_keys, preferred_element_type=jnp.float32)
        * softmax_scale
    )
    position = start + jnp.arange(row_count, dtype=jnp.int32)
    visible = jnp.arange(key_count, dtype=jnp.int32)[None, :] <= position[:, None]
    scores = jnp.where(visible[None], scores, -jnp.inf)
    row_max = jnp.max(scores, axis=-1, keepdims=True)
    exp_scores = jnp.exp(scores - row_max)
    attention = exp_scores / jnp.sum(exp_scores, axis=-1, keepdims=True)
    attention_low = attention.astype(jnp.bfloat16)
    out_latent = jnp.einsum(
        "hqk,kr->hqr", attention_low, latent, preferred_element_type=jnp.float32
    )
    grad_split = grad_rows.reshape(row_count, head_count, VDIM)
    grad_latent = jnp.einsum(
        "qhv,hrv->hqr", grad_split, value_up, preferred_element_type=jnp.float32
    )
    grad_latent_low = grad_latent.astype(jnp.bfloat16)
    row_delta = jnp.sum(grad_latent * out_latent, axis=-1, keepdims=True)
    grad_attention = jnp.einsum(
        "hqr,kr->hqk", grad_latent_low, latent, preferred_element_type=jnp.float32
    )
    grad_scores = (attention * (grad_attention - row_delta) * softmax_scale).astype(jnp.bfloat16)
    grad_full = jnp.einsum("hqk,kc->hqc", grad_scores, seq_keys, preferred_element_type=jnp.float32)
    grad_qlat = grad_full[..., :RANK].astype(jnp.bfloat16)
    grad_nope = jnp.einsum("hqr,hrd->qhd", grad_qlat, key_up, preferred_element_type=jnp.float32)
    grad_rope = jnp.transpose(grad_full[..., RANK:], (1, 0, 2))
    grad_query = jnp.concatenate([grad_nope, grad_rope], axis=-1)
    grad_query = grad_query.reshape(row_count, head_count * (NOPE + ROPE)).astype(jnp.bfloat16)
    grad_keys = jnp.einsum(
        "hqk,hqc->kc", grad_scores, query_full, preferred_element_type=jnp.float32
    )
    grad_values = jnp.einsum(
        "hqk,hqr->kr", attention_low, grad_latent_low, preferred_element_type=jnp.float32
    )
    grad_keys = grad_keys + jnp.pad(grad_values, ((0, 0), (0, ROPE)))
    grad_key_up = jnp.einsum(
        "hqr,qhd->hrd", grad_qlat, query_nope, preferred_element_type=jnp.float32
    )
    grad_value_up = jnp.einsum(
        "hqr,qhv->hrv",
        out_latent.astype(jnp.bfloat16),
        grad_split,
        preferred_element_type=jnp.float32,
    )
    return (grad_query, grad_keys, grad_key_up, grad_value_up)


def local(queries, grad_out, cache_codes, cache_exponents, page_table, offsets, key_up, value_up):
    query_count = queries.shape[2]
    key_pool = lax.all_gather(
        dequantize(cache_codes, cache_exponents), ("sa", "sb"), axis=1, tiled=True
    )
    seq_total = page_table.shape[1]
    seq_keys = key_pool[0][page_table[0]].reshape(seq_total, -1, RANK + ROPE)
    moved = (
        lax.all_to_all(queries, ("sa", "sb"), split_axis=3, concat_axis=1, tiled=True),
        lax.all_to_all(grad_out, ("sa", "sb"), split_axis=3, concat_axis=1, tiled=True),
    )
    head_queries = moved[0][0]
    head_grads = moved[1][0]
    block = min(8, seq_total)
    rounds = seq_total // block

    def to_blocks(array):
        return array.reshape((rounds, block) + array.shape[1:])

    batched = jax.vmap(sequence_grads, in_axes=(0, 0, 0, 0, None, None))

    def seq_step(totals, inputs):
        results = batched(inputs[0], inputs[1], inputs[2], inputs[3], key_up, value_up)
        return (
            (totals[0] + jnp.sum(results[2], axis=0), totals[1] + jnp.sum(results[3], axis=0)),
            (results[0], results[1]),
        )

    zero_sums = (jnp.zeros(key_up.shape, jnp.float32), jnp.zeros(value_up.shape, jnp.float32))
    block_inputs = (
        to_blocks(head_queries),
        to_blocks(head_grads),
        to_blocks(seq_keys),
        to_blocks(offsets[0]),
    )
    weight_sums, outputs = lax.scan(seq_step, zero_sums, block_inputs)
    grad_rows = outputs[0].reshape(seq_total, query_count, -1)
    token_rows = lax.all_to_all(
        grad_rows[None], ("sa", "sb"), split_axis=1, concat_axis=3, tiled=True
    )
    key_pages = outputs[1].reshape(-1, PAGE, RANK + ROPE)
    flat_table = page_table[0].reshape(-1)
    cache_term = jnp.zeros(key_pages.shape, jnp.float32).at[flat_table].set(key_pages)[None]
    grad_cache = lax.psum_scatter(
        cache_term.astype(jnp.bfloat16), ("sa", "sb"), scatter_dimension=1, tiled=True
    ).astype(jnp.float32)
    grad_key_up, grad_value_up = (
        lax.psum(weight_sums[0].astype(jnp.bfloat16), "rep").astype(jnp.float32),
        lax.psum(weight_sums[1].astype(jnp.bfloat16), "rep").astype(jnp.float32),
    )
    return (token_rows, grad_cache, grad_key_up, grad_value_up)


def solution(mesh):
    in_specs = (
        P("rep", ("sa", "sb"), None, None),
        P("rep", ("sa", "sb"), None, None),
        P("rep", ("sa", "sb"), None, None),
        P("rep", ("sa", "sb"), None, None),
        P("rep", None, None),
        P("rep", None),
        P(("sa", "sb"), None, None),
        P(("sa", "sb"), None, None),
    )
    out_specs = (
        P("rep", ("sa", "sb"), None, None),
        P("rep", ("sa", "sb"), None, None),
        P(("sa", "sb"), None, None),
        P(("sa", "sb"), None, None),
    )
    return jax.shard_map(local, mesh=mesh, in_specs=in_specs, out_specs=out_specs, check_vma=False)
```

profile of v0, /device:TPU:0, one launch (start us, length us, event | category | flops | bytes accessed | tf_op | source)
XLA Modules:
  0.0 905.1 jit_solution(5733547862314508015)
XLA Ops:
  7.2 12.7 %copy.82 = bf16[1,4,64,8192]{2,1,0,3:T(4,128)(2,1)} copy(bf16[1,4,64,8192]{3,2,1,0:T(8,128)(2,1)} %param.11) | data formatting | bytes 8388608 | tf_op args[1]
  19.9 14.0 %reshape.179 = bf16[16,2,65536]{2,1,0:T(2,128)(2,1)} reshape(bf16[8192,1,4,64]{3,2,1,0:T(4,128)(2,1)} %bitcast.155) | data formatting | bytes 8388608
  33.8 7.4 all-to-all-start.1
  41.3 18.5 %copy.76 = bf16[1,4,64,12288]{2,1,0,3:T(4,128)(2,1)} copy(bf16[1,4,64,12288]{3,2,1,0:T(8,128)(2,1)} %param.10) | data formatting | bytes 12582912 | tf_op args[0]
  59.7 16.7 %reshape.177 = bf16[16,2,98304]{2,1,0:T(2,128)(2,1)} reshape(bf16[12288,1,4,64]{3,2,1,0:T(4,128)(2,1)} %bitcast.153) | data formatting | bytes 12582912
  76.4 42.5 %all-to-all-done.1 = bf16[16,2,65536]{2,1,0:T(2,128)(2,1)} async-done(((bf16[16,2,65536]{2,1,0:T(2,128)(2,1)}), bf16[16,2,65536]{2,1,0:T(2,128)(2,1)}, u32[]{:S(2)}, u32[]{:S(2)}) %all-to-all-start.1) | async-done | bytes 4194336 | tf_op jit(solution)/shard_map/all_to_all | solution.py:91
  118.9 19.7 %all-to-all-start = ((bf16[16,2,98304]{2,1,0:T(2,128)(2,1)}), bf16[16,2,98304]{2,1,0:T(2,128)(2,1)}, u32[]{:S(2)}, u32[]{:S(2)}) async-start(bf16[16,2,98304]{2,1,0:T(2,128)(2,1)} %reshape.177), calls=%async_computation | async-start | bytes 12582912 | tf_op jit(solution)/shard_map/all_to_all | solution.py:90
  142.2 13.7 %reshape.180 = bf16[8192,1,4,64]{3,2,1,0:T(4,128)(2,1)} reshape(bf16[16,2,65536]{2,1,0:T(2,128)(2,1)} %all-to-all-done.1) | data formatting | bytes 8388608
  155.9 12.7 %copy.83 = bf16[1,16,4,64,512]{4,3,2,1,0:T(8,128)(2,1)} copy(bf16[1,16,4,64,512]{3,2,4,1,0:T(4,128)(2,1)} %bitcast.154) | data formatting | bytes 8388608 | tf_op jit(solution)/shard_map/all_to_all | solution.py:91
  168.6 111.1 %all-gather.2.cloned.1.call-done = bf16[1,320,16,576]{3,2,0,1:T(8,128)(2,1)} async-done(((bf16[1,20,16,576]{3,2,0,1:T(8,128)(2,1)}), bf16[1,320,16,576]{3,2,0,1:T(8,128)(2,1)}) %all-gather.2.cloned.1.call-update) | async-done | bytes 5898256 | tf_op jit(solution)/shard_map/all_gather | solution.py:84
  279.8 17.0 %gather_fusion = bf16[320,16,576]{2,1,0:T(8,128)(2,1)} fusion(bf16[320,16,576]{2,1,0:T(8,128)(2,1)} %bitcast.162, s32[1024]{0:T(1024)S(1)} %pad_clamp_fusion), kind=kCustom, calls=%fused_computation | custom fusion | bytes 11797760 | tf_op jit(solution)/shard_map/gather | solution.py:88
  296.8 16.3 %reshape.178 = bf16[12288,1,4,64]{3,2,1,0:T(4,128)(2,1)} reshape(bf16[16,2,98304]{2,1,0:T(2,128)(2,1)} %all-to-all-done) | data formatting | bytes 12582912
  313.1 18.0 %copy.77 = bf16[1,16,4,64,768]{4,3,2,1,0:T(8,128)(2,1)} copy(bf16[1,16,4,64,768]{3,2,4,1,0:T(4,128)(2,1)} %bitcast.152) | data formatting | bytes 12582912 | tf_op jit(solution)/shard_map/all_to_all | solution.py:90
  331.2 357.1 %while.19 = (s32[]{:T(128)}, f32[4,512,128]{2,1,0:T(8,128)}, f32[4,512,128]{2,1,0:T(8,128)}, bf16[8,8,64,768]{3,2,1,0:T(8,128)(2,1)}, f32[8,8,80,576]{3,2,1,0:T(...) while((s32[]{:T(128)}, f32[4,512,128]{2,1,0:T(8,128)}, ...), condition=%wide.region_4.5_spmd.clone, body=%wide.region_0.4_spmd.clone.sunk | while | flops 2433338112 | bytes 152711936 | solution.py:117
  334.7 3.3 fusion.139
  340.5 2.6 fusion.141
  344.5 5.7 fusion.143
  350.2 4.0 fusion.144
  365.0 7.4 fusion.149
  372.5 3.3 bitcast_dynamic-update-slice_fusion.2
  379.3 3.3 fusion.139
  385.1 2.6 fusion.141
  389.1 5.7 fusion.143
  394.8 4.0 fusion.144
  409.7 7.4 fusion.149
  417.1 3.3 bitcast_dynamic-update-slice_fusion.2
  423.9 3.3 fusion.139
  433.7 5.7 fusion.143
  439.4 4.0 fusion.144
  454.2 7.4 fusion.149
  461.7 3.3 bitcast_dynamic-update-slice_fusion.2
  468.5 3.3 fusion.139
  478.3 5.7 fusion.143
  484.0 4.0 fusion.144
  498.9 7.4 fusion.149
  506.3 3.4 bitcast_dynamic-update-slice_fusion.2
  513.2 3.3 fusion.139
  523.0 5.7 fusion.143
  528.7 4.0 fusion.144
  543.5 7.4 fusion.149
  551.0 3.3 bitcast_dynamic-update-slice_fusion.2
  557.8 3.3 fusion.139
  567.6 5.7 fusion.143
  573.3 4.0 fusion.144
  588.1 7.4 fusion.149
  595.6 3.4 bitcast_dynamic-update-slice_fusion.2
  602.5 3.3 fusion.139
  608.3 2.6 fusion.141
  612.2 5.7 fusion.143
  618.0 4.0 fusion.144
  632.8 7.4 fusion.149
  640.2 3.3 bitcast_dynamic-update-slice_fusion.2
  647.1 3.3 fusion.139
  652.9 2.6 fusion.141
  656.8 5.7 fusion.143
  662.5 4.0 fusion.144
  677.4 7.4 fusion.149
  684.8 3.4 bitcast_dynamic-update-slice_fusion.2
  688.2 23.8 %all-to-all-start.2 = ((bf16[1,64,64,768]{3,2,0,1:T(8,128)(2,1)}), bf16[1,64,64,768]{3,2,0,1:T(8,128)(2,1)}, u32[]{:S(2)}, u32[]{:S(2)}) async-start(bf16[1,64,64,768]{3,2,0,1:T(8,128)(2,1)} %bitcast.163), calls=%async_computation.2 | async-start | bytes 12582912 | tf_op jit(solution)/shard_map/all_to_all | solution.py:119
  714.1 5.5 broadcast_in_dim.57
  719.6 50.5 %scatter_fusion = f32[320,16,576]{2,1,0:T(8,128)} fusion(f32[320,16,576]{2,1,0:T(8,128)} %broadcast_in_dim.57, s32[320]{0:T(512)S(1)} %fusion.72, f32[320,16,576]{2,1,0:T(8,128)} %bitcast.158), kind=kCustom, calls=%fused_computation.1 | custom fusion | bytes 35390720 | tf_op jit(solution)/shard_map/scatter | solution.py:124
  770.1 8.1 convert_bitcast_fusion.1
  782.4 107.9 %reduce-scatter.2.cloned.1.call-done = bf16[1,20,16,576]{3,2,1,0:T(8,128)(2,1)} async-done(((bf16[1,320,16,576]{3,2,1,0:T(8,128)(2,1)}), bf16[1,20,16,576]{3,2,1,0:T(8,128)(2,1)}) %reduce-scatter.2.cloned.1.call-update) | async-done | bytes 368656 | tf_op jit(solution)/shard_map/reduce_scatter | solution.py:125
  892.3 6.3 copy.95
  (495 shorter events, 165.4 us)
Async XLA Ops:
  33.8 85.1 %all-to-all-start.1 = ((bf16[16,2,65536]{2,1,0:T(2,128)(2,1)}), bf16[16,2,65536]{2,1,0:T(2,128)(2,1)}, u32[]{:S(2)}, u32[]{:S(2)}) async-start(bf16[16,2,65536]{2,1,0:T(2,128)(2,1)} %reshape.179), calls=%async_computation.1 | async-start | bytes 8388608 | tf_op jit(solution)/shard_map/all_to_all | solution.py:91
  76.4 62.3 %copy-start.19 = (bf16[1,20,16,576]{3,2,1,0:T(8,128)(2,1)S(1)}, bf16[1,20,16,576]{3,2,1,0:T(8,128)(2,1)}, u32[]{:S(2)}) copy-start(bf16[1,20,16,576]{3,2,1,0:T(8,128)(2,1)} %param.12) | copy-start | bytes 1105924
  76.4 62.3 %copy-start.20 = (s32[1,20,16,4]{1,3,2,0:T(4,128)S(1)}, s32[1,20,16,4]{1,3,2,0:T(4,128)}, u32[]{:S(2)}) copy-start(s32[1,20,16,4]{1,3,2,0:T(4,128)} %param.13) | copy-start | bytes 15364
  118.9 177.9 %all-to-all-start = ((bf16[16,2,98304]{2,1,0:T(2,128)(2,1)}), bf16[16,2,98304]{2,1,0:T(2,128)(2,1)}, u32[]{:S(2)}, u32[]{:S(2)}) async-start(bf16[16,2,98304]{2,1,0:T(2,128)(2,1)} %reshape.177), calls=%async_computation | async-start | bytes 12582912 | tf_op jit(solution)/shard_map/all_to_all | solution.py:90
  138.7 141.1 %all-gather.2.cloned.1.call-start = ((), (), s32[]{:S(2)}) async-start(), calls=%async_computation.4 | async-start | bytes 6963200 | tf_op jit(solution)/shard_map/all_gather | solution.py:84
  313.1 18.1 %copy-start.9 = (bf16[4,512,128]{2,1,0:T(8,128)(2,1)S(1)}, bf16[4,512,128]{2,1,0:T(8,128)(2,1)}, u32[]{:S(2)}) copy-start(bf16[4,512,128]{2,1,0:T(8,128)(2,1)} %param.17) | copy-start | bytes 1572868
  334.7 5.1 copy-start.14
  343.1 11.1 %copy-start.7 = (f32[8,4,64,80]{3,2,1,0:T(8,128)}, f32[8,4,64,80]{3,2,1,0:T(8,128)S(1)}, u32[]{:S(2)}) copy-start(f32[8,4,64,80]{3,2,1,0:T(8,128)S(1)} %fusion.141) | copy-start | bytes 1966084 | tf_op jit(solution)/shard_map/while
  350.2 4.3 copy-start.8
  355.5 4.3 copy-start
  355.5 4.3 copy-start.4
  364.1 8.4 copy-start.12
  365.0 7.4 copy-start.3
  379.3 5.1 copy-start.14
  387.8 11.1 %copy-start.7 = (f32[8,4,64,80]{3,2,1,0:T(8,128)}, f32[8,4,64,80]{3,2,1,0:T(8,128)S(1)}, u32[]{:S(2)}) copy-start(f32[8,4,64,80]{3,2,1,0:T(8,128)S(1)} %fusion.141) | copy-start | bytes 1966084 | tf_op jit(solution)/shard_map/while
  394.8 4.3 copy-start.8
  400.1 4.3 copy-start
  400.1 4.3 copy-start.4
  408.7 8.4 copy-start.12
  409.6 7.4 copy-start.3
  423.9 5.1 copy-start.14
  432.4 11.1 %copy-start.7 = (f32[8,4,64,80]{3,2,1,0:T(8,128)}, f32[8,4,64,80]{3,2,1,0:T(8,128)S(1)}, u32[]{:S(2)}) copy-start(f32[8,4,64,80]{3,2,1,0:T(8,128)S(1)} %fusion.141) | copy-start | bytes 1966084 | tf_op jit(solution)/shard_map/while
  439.4 4.3 copy-start.8
  444.7 4.3 copy-start
  444.7 4.3 copy-start.4
  453.3 8.4 copy-start.12
  454.2 7.4 copy-start.3
  468.5 5.1 copy-start.14
  477.0 11.1 %copy-start.7 = (f32[8,4,64,80]{3,2,1,0:T(8,128)}, f32[8,4,64,80]{3,2,1,0:T(8,128)S(1)}, u32[]{:S(2)}) copy-start(f32[8,4,64,80]{3,2,1,0:T(8,128)S(1)} %fusion.141) | copy-start | bytes 1966084 | tf_op jit(solution)/shard_map/while
  489.3 4.3 copy-start
  489.3 4.3 copy-start.4
  497.9 8.4 copy-start.12
  498.9 7.4 copy-start.3
  513.2 5.1 copy-start.14
  521.6 11.1 %copy-start.7 = (f32[8,4,64,80]{3,2,1,0:T(8,128)}, f32[8,4,64,80]{3,2,1,0:T(8,128)S(1)}, u32[]{:S(2)}) copy-start(f32[8,4,64,80]{3,2,1,0:T(8,128)S(1)} %fusion.141) | copy-start | bytes 1966084 | tf_op jit(solution)/shard_map/while
  528.7 4.3 copy-start.8
  534.0 4.3 copy-start
  534.0 4.3 copy-start.4
  542.6 8.4 copy-start.12
  543.5 7.4 copy-start.3
  557.8 5.1 copy-start.14
  566.3 11.1 %copy-start.7 = (f32[8,4,64,80]{3,2,1,0:T(8,128)}, f32[8,4,64,80]{3,2,1,0:T(8,128)S(1)}, u32[]{:S(2)}) copy-start(f32[8,4,64,80]{3,2,1,0:T(8,128)S(1)} %fusion.141) | copy-start | bytes 1966084 | tf_op jit(solution)/shard_map/while
  578.6 4.3 copy-start
  578.6 4.3 copy-start.4
  587.2 8.4 copy-start.12
  588.1 7.4 copy-start.3
  602.5 5.1 copy-start.14
  610.9 11.1 %copy-start.7 = (f32[8,4,64,80]{3,2,1,0:T(8,128)}, f32[8,4,64,80]{3,2,1,0:T(8,128)S(1)}, u32[]{:S(2)}) copy-start(f32[8,4,64,80]{3,2,1,0:T(8,128)S(1)} %fusion.141) | copy-start | bytes 1966084 | tf_op jit(solution)/shard_map/while
  623.2 4.3 copy-start
  623.2 4.3 copy-start.4
  631.8 8.4 copy-start.12
  632.8 7.4 copy-start.3
  647.0 5.1 copy-start.14
  655.5 11.1 %copy-start.7 = (f32[8,4,64,80]{3,2,1,0:T(8,128)}, f32[8,4,64,80]{3,2,1,0:T(8,128)S(1)}, u32[]{:S(2)}) copy-start(f32[8,4,64,80]{3,2,1,0:T(8,128)S(1)} %fusion.141) | copy-start | bytes 1966084 | tf_op jit(solution)/shard_map/while
  667.8 4.3 copy-start
  667.8 4.3 copy-start.4
  676.4 8.4 copy-start.12
  677.4 7.4 copy-start.3
  688.2 23.8 %copy-start.22 = (s32[1,64,5]{1,0,2:T(1,128)S(1)}, s32[1,64,5]{1,0,2:T(1,128)}, u32[]{:S(2)}) copy-start(s32[1,64,5]{1,0,2:T(1,128)} %param.14) | copy-start | bytes 3844
  688.2 24.1 %copy-start.18 = (f32[4,512,128]{2,1,0:T(8,128)S(1)}, f32[4,512,128]{2,1,0:T(8,128)}, u32[]{:S(2)}) copy-start(f32[4,512,128]{2,1,0:T(8,128)} %get-tuple-element.339) | copy-start | bytes 3145732
  688.2 25.0 %copy-start.6 = (f32[4,512,128]{2,1,0:T(8,128)S(1)}, f32[4,512,128]{2,1,0:T(8,128)}, u32[]{:S(2)}) copy-start(f32[4,512,128]{2,1,0:T(8,128)} %get-tuple-element.340) | copy-start | bytes 3145732
  688.2 204.1 %all-to-all-start.2 = ((bf16[1,64,64,768]{3,2,0,1:T(8,128)(2,1)}), bf16[1,64,64,768]{3,2,0,1:T(8,128)(2,1)}, u32[]{:S(2)}, u32[]{:S(2)}) async-start(bf16[1,64,64,768]{3,2,0,1:T(8,128)(2,1)} %bitcast.163), calls=%async_computation.2 | async-start | bytes 12582912 | tf_op jit(solution)/shard_map/all_to_all | solution.py:119
  712.0 66.3 %all-reduce.4.cloned.1.call-start = ((), (), s32[]{:S(2)}) async-start(), calls=%async_computation.6 | async-start | bytes 2097152 | tf_op jit(solution)/shard_map/psum | solution.py:129
  714.1 176.2 %reduce-scatter.2.cloned.1.call-start = ((), (), s32[]{:S(2)}) async-start(), calls=%async_computation.5 | async-start | bytes 6963200 | tf_op jit(solution)/shard_map/reduce_scatter | solution.py:125
  (78 other events, 219.1 us)
Sparse Core Ops, SparseCore 0:
  142.3 137.3 all-gather.1
  715.8 41.5 all-reduce.3
  778.4 111.9 reduce-scatter.1
where the time goes:
time: 911 us; the launch traced here: 905 us
  local copies, waits for them, and re-layouts  278 us (31%)
  waiting for transfers between devices  262 us (29%)
  matrix products  234 us (26%)
  other arithmetic  64 us (7%)
  starting transfers between devices  51 us (6%)
  between operations  14 us (2%)
    all_gather x1, waiting for transfers between devices, local(): lax.all_gather(dequantize(cache_codes, cache_exponents), ('sa', 'sb'), ax...  111 us
    reduce_scatter x1, waiting for transfers between devices, local(): lax.psum_scatter(cache_term.astype(jnp.bfloat16), ('sa', 'sb'), scatter_d...  108 us
    unnamed x24, local copies, waits for them, and re-layouts  92.5 us
    dot_general x8, matrix products, sequence_grads(): jnp.einsum('hqk,hqr->kr', attention_low, grad_latent_low, preferred_eleme...  59.4 us
    scatter x1, local copies, waits for them, and re-layouts, local(): jnp.zeros(key_pages.shape, jnp.float32).at[flat_table].set(key_pages)[None]  50.5 us
    dot_general x8, matrix products, sequence_grads(): jnp.einsum('hqk,kr->hqr', attention_low, latent, preferred_element_type=j...  45.7 us
    all_to_all x1, waiting for transfers between devices, local(): lax.all_to_all(grad_out, ('sa', 'sb'), split_axis=3, concat_axis=1, tiled...  42.5 us
    reduce_sum x8, other arithmetic, sequence_grads(): row_delta = jnp.sum(grad_latent * out_latent, axis=-1, keepdims=True)  32.3 us
  transfers between devices with their start and end apart: 6, of which 3 were waited for; matrix products, arithmetic and copies ran while one was open for 17% of the time, Pallas kernels for 0%

commit v1 on v0

v1 whole, which is shorter than its diff:
```python
import functools

import jax
import jax.numpy as jnp
from jax import lax
from jax.experimental import pallas as pl
from jax.experimental.pallas import tpu as pltpu
from jax.sharding import PartitionSpec as P

LANES = 128
NT = (((1,), (1,)), ((), ()))
TN = (((0,), (0,)), ((), ()))


def dequantize(stored, exponents, rank):
    block_size = rank // exponents.shape[-1]
    factor = jnp.repeat(jnp.exp2(exponents.astype(jnp.float32)), block_size, axis=-1)
    latent = (stored[..., :rank].astype(jnp.float32) * factor).astype(jnp.bfloat16)
    return jnp.concatenate([latent, stored[..., rank:]], axis=-1)


def matmul(a, b, dims=None):
    if dims is None:
        return jnp.dot(a, b, preferred_element_type=jnp.float32)
    return lax.dot_general(a, b, dims, preferred_element_type=jnp.float32)


def pair_kernel(
    softmax_scale, offset_ref, q_ref, g_ref, w_ref, lat_ref, lat_t_ref, rope_ref,
    base_lat_ref, base_rope_ref, filled_ref,
    dq_ref, dw_ref, dlat_ref, drope_ref, kv_scratch, grad_scratch,
):
    seqs, rows, width = q_ref.shape
    keys = lat_ref.shape[0] // seqs
    half = LANES // 2

    @pl.when(pl.program_id(0) == 0)
    def _():
        dlat_ref[...] = base_lat_ref[...]
        drope_ref[...] = base_rope_ref[...]

    weights = w_ref[0]
    kv = matmul(lat_ref[...], weights)
    low = lax.broadcasted_iota(jnp.int32, (lat_ref.shape[0], LANES), 1) < half
    rope = rope_ref[...]
    turned = pltpu.roll(kv[:, LANES : 2 * LANES], half, 1)
    kv_scratch[:, :LANES] = kv[:, :LANES].astype(jnp.bfloat16)
    kv_scratch[:, LANES : 2 * LANES] = jnp.where(low, rope, turned).astype(jnp.bfloat16)
    kv_scratch[:, 2 * LANES : width] = jnp.where(low, turned, rope).astype(jnp.bfloat16)
    kv_scratch[:, width:] = kv[:, 2 * LANES :].astype(jnp.bfloat16)

    lane_q = lax.broadcasted_iota(jnp.int32, (rows, width), 1) < width // 2
    key_at = lax.broadcasted_iota(jnp.int32, (keys, 2 * rows), 0)
    lane = lax.broadcasted_iota(jnp.int32, (keys, 2 * rows), 1)
    query_at = jnp.where(lane < rows, lane, lane - rows)
    zero_g = jnp.zeros((rows, LANES), jnp.bfloat16)
    for s in range(seqs):
        span = slice(s * keys, (s + 1) * keys)
        q = q_ref[s]
        zero_q = jnp.zeros_like(q)
        q_two = jnp.concatenate([jnp.where(lane_q, q, zero_q), jnp.where(lane_q, zero_q, q)], axis=0)
        g = g_ref[s]
        g_two = jnp.concatenate(
            [
                jnp.concatenate([g[:, :LANES], zero_g], axis=1),
                jnp.concatenate([zero_g, g[:, LANES:]], axis=1),
            ],
            axis=0,
        )
        k = kv_scratch[span, :width]
        v = kv_scratch[span, width:]
        scores = matmul(k, q_two, NT) * softmax_scale
        visible = key_at <= query_at + offset_ref[s]
        scores = jnp.where(visible, scores, -jnp.inf)
        exp_scores = jnp.exp(scores - jnp.max(scores, axis=0, keepdims=True))
        attention = exp_scores / jnp.sum(exp_scores, axis=0, keepdims=True)
        attention_low = attention.astype(jnp.bfloat16)
        grad_attention = matmul(v, g_two, NT)
        row_delta = jnp.sum(attention_low.astype(jnp.float32) * grad_attention, axis=0, keepdims=True)
        grad_scores = (attention * (grad_attention - row_delta) * softmax_scale).astype(jnp.bfloat16)
        dq = matmul(grad_scores, k, TN)
        dq_ref[s] = jnp.where(lane_q, dq[:rows], dq[rows:]).astype(jnp.bfloat16)
        dk = matmul(grad_scores, q_two)
        dv = matmul(attention_low, g_two)
        low_s = low[:keys]
        first, middle, last = dk[:, :LANES], dk[:, LANES : 2 * LANES], dk[:, 2 * LANES :]
        drope_ref[span, :] += jnp.where(low_s, middle, last)
        second = pltpu.roll(jnp.where(low_s, last, middle), half, 1)
        grad_scratch[span, :LANES] = first.astype(jnp.bfloat16)
        grad_scratch[span, LANES : 2 * LANES] = second.astype(jnp.bfloat16)
        grad_scratch[span, 2 * LANES :] = dv.astype(jnp.bfloat16)
    grads = grad_scratch[...]
    dlat_ref[...] += matmul(grads, weights, NT)
    dw_ref[0] = matmul(lat_t_ref[...], grads).astype(jnp.bfloat16)


def pair_grads(offsets, queries, grads, weights, lat, lat_t, rope2, base_lat, base_rope, filled, chunk, chunks):
    owners, rank, columns = weights.shape
    seqs, rows, _ = queries.shape
    key_rows = lat.shape[0]
    width = queries.shape[2] // (owners * chunks)
    v_width = grads.shape[2] // (owners * chunks)
    softmax_scale = (width // 2) ** (-0.5)
    whole = lambda i, off: (0, 0)
    rows_of = lambda i, off: (0, 0, i * chunks + chunk)
    return pl.pallas_call(
        functools.partial(pair_kernel, softmax_scale),
        grid_spec=pltpu.PrefetchScalarGridSpec(
            num_scalar_prefetch=1,
            grid=(owners,),
            in_specs=[
                pl.BlockSpec((seqs, rows, width), rows_of),
                pl.BlockSpec((seqs, rows, v_width), rows_of),
                pl.BlockSpec((1, rank, columns), lambda i, off: (i, 0, 0)),
                pl.BlockSpec((key_rows, rank), whole),
                pl.BlockSpec((rank, key_rows), whole),
                pl.BlockSpec((key_rows, LANES), whole),
                pl.BlockSpec((key_rows, rank), whole),
                pl.BlockSpec((key_rows, LANES), whole),
                pl.BlockSpec(memory_space=pl.ANY),
            ],
            out_specs=[
                pl.BlockSpec((seqs, rows, width), rows_of),
                pl.BlockSpec((1, rank, columns), lambda i, off: (i, 0, 0)),
                pl.BlockSpec((key_rows, rank), whole),
                pl.BlockSpec((key_rows, LANES), whole),
            ],
            scratch_shapes=[
                pltpu.VMEM((key_rows, width + v_width), jnp.bfloat16),
                pltpu.VMEM((key_rows, columns), jnp.bfloat16),
            ],
        ),
        out_shape=[
            jax.ShapeDtypeStruct(queries.shape, jnp.bfloat16),
            jax.ShapeDtypeStruct(weights.shape, jnp.bfloat16),
            jax.ShapeDtypeStruct((key_rows, rank), jnp.float32),
            jax.ShapeDtypeStruct((key_rows, LANES), jnp.float32),
        ],
        input_output_aliases={9: 0} if chunk else {},
        compiler_params=pltpu.CompilerParams(vmem_limit_bytes=40 * 2**20),
        cost_estimate=pl.CostEstimate(
            flops=owners * 2 * (3 * key_rows * rank * columns + key_rows * 2 * rows * (3 * width + 2 * v_width)),
            bytes_accessed=owners * (2 * seqs * rows * (2 * width + v_width) + 4 * rank * columns),
            transcendentals=owners * key_rows * 2 * rows,
        ),
        name=f"pair_grads_{chunk}",
    )(offsets, queries, grads, weights, lat, lat_t, rope2, base_lat, base_rope, filled)


def local(queries, grad_out, cache_codes, cache_exponents, page_table, offsets, key_up, value_up):
    axes = ("sa", "sb")
    heads, rank, nope = key_up.shape
    _, seqs, rows, _ = queries.shape
    pages, page, full = cache_codes.shape[1:]
    rope_width = full - rank
    me = lax.axis_index(axes)
    chunks = heads // 2

    pool = lax.all_gather(dequantize(cache_codes, cache_exponents, rank)[0], axes, axis=0, tiled=True)
    gathered = []
    for c in range(chunks):
        block = jnp.concatenate(
            [key_up[2 * c], key_up[2 * c + 1], value_up[2 * c], value_up[2 * c + 1]], axis=1
        )
        gathered.append(lax.all_gather(block, axes, axis=0, tiled=False))

    table = page_table[0].reshape(-1)
    own = lax.dynamic_slice_in_dim(table, me * pages, pages)
    inverse = jnp.zeros_like(table).at[table].set(jnp.arange(table.shape[0], dtype=table.dtype))
    own_inverse = lax.dynamic_slice_in_dim(inverse, me * pages, pages)
    my_offsets = lax.dynamic_slice_in_dim(offsets[0], me * seqs, seqs)

    keys = pool[own].reshape(pages * page, full)
    lat = keys[:, :rank]
    lat_t = lat.T
    rope = keys[:, rank:].astype(jnp.float32)
    rope2 = jnp.concatenate([rope, rope], axis=1)
    grad_lat = jnp.zeros((pages * page, rank), jnp.float32)
    grad_rope = jnp.zeros((pages * page, 2 * rope_width), jnp.float32)
    grad_queries = queries[0]
    weight_parts = []
    for c in range(chunks):
        grad_queries, dw, grad_lat, grad_rope = pair_grads(
            my_offsets, queries[0], grad_out[0], gathered[c], lat, lat_t, rope2, grad_lat, grad_rope,
            grad_queries, c, chunks
        )
        mine = lax.psum_scatter(dw, axes, scatter_dimension=0, tiled=True)
        weight_parts.append(lax.psum(mine[0], "rep").astype(jnp.float32))

    grad_keys = jnp.concatenate(
        [grad_lat, grad_rope[:, :rope_width] + grad_rope[:, rope_width:]], axis=1
    ).astype(jnp.bfloat16)
    all_pages = lax.all_gather(grad_keys.reshape(pages, page, full), axes, axis=0, tiled=True)
    grad_cache = all_pages[own_inverse].astype(jnp.float32)[None]
    split = [part.reshape(rank, 4, nope) for part in weight_parts]
    grad_key_up = jnp.stack([part[:, i] for part in split for i in (0, 1)])
    grad_value_up = jnp.stack([part[:, i] for part in split for i in (2, 3)])
    return (grad_queries[None], grad_cache, grad_key_up, grad_value_up)


def solution(mesh):
    in_specs = (
        P("rep", ("sa", "sb"), None, None),
        P("rep", ("sa", "sb"), None, None),
        P("rep", ("sa", "sb"), None, None),
        P("rep", ("sa", "sb"), None, None),
        P("rep", None, None),
        P("rep", None),
        P(("sa", "sb"), None, None),
        P(("sa", "sb"), None, None),
    )
    out_specs = (
        P("rep", ("sa", "sb"), None, None),
        P("rep", ("sa", "sb"), None, None),
        P(("sa", "sb"), None, None),
        P(("sa", "sb"), None, None),
    )
    return jax.shard_map(local, mesh=mesh, in_specs=in_specs, out_specs=out_specs, check_vma=False)
```

time: 911 us -> 610 us (0.67)
  local copies, waits for them, and re-layouts: 278 us -> 28 us
  matrix products: 234 us -> 0 us
  waiting for transfers between devices: 262 us -> 469 us
  Pallas kernels: 0 us -> 87.7 us
  other arithmetic: 64 us -> 10.8 us
  starting transfers between devices: 51 us -> 0.29 us
    dot_general x88 -> x0, matrix products: 234 us -> none  [the longest x8 59.4 us: sequence_grads(): jnp.einsum('hqk,hqr->kr', attention_low, grad_latent_low, preferred_eleme...]
    all_gather x1 -> x4, waiting for transfers between devices: 111 us -> 223 us  [the longest x2 99.7 us: local(): gathered.append(lax.all_gather(block, axes, axis=0, tiled=False))]
    reduce_scatter x1 -> x2, waiting for transfers between devices: 108 us -> 208 us  [local(): mine = lax.psum_scatter(dw, axes, scatter_dimension=0, tiled=True)]
    pallas_call x0 -> x2, Pallas kernels: none -> 87.7 us  [pair_grads(): pl.pallas_call(functools.partial(pair_kernel, softmax_scale), grid_spec=p...]
    unnamed x24 -> x15, local copies, waits for them, and re-layouts: 92.5 us -> 10.1 us
    all_to_all x3 -> x0, starting transfers between devices: 50.9 us -> none  [the longest x1 23.8 us: local(): lax.all_to_all(grad_rows[None], ('sa', 'sb'), split_axis=1, concat_axis=3...]
    scatter x1, local copies, waits for them, and re-layouts: 50.5 us -> 2.91 us  [local(): jnp.zeros_like(table).at[table]]
    all_to_all x3 -> x0, waiting for transfers between devices: 42.5 us -> none  [the longest x1 42.5 us: local(): lax.all_to_all(grad_out, ('sa', 'sb'), split_axis=3, concat_axis=1, tiled...]
  transfers between devices with their start and end apart: 6 -> 7, of which waited for: 3 -> 7; matrix products, arithmetic and copies ran while one was open for 17% -> 3% of each run, Pallas kernels for 0% -> 7%
where the time goes in v1:
time: 610 us
  waiting for transfers between devices  469 us (77%)
  Pallas kernels  87.7 us (14%)
  local copies, waits for them, and re-layouts  28 us (5%)
  between operations  14.3 us (2%)
  other arithmetic  10.8 us (2%)
    reduce_scatter x2, waiting for transfers between devices, local(): mine = lax.psum_scatter(dw, axes, scatter_dimension=0, tiled=True)  208 us
    all_gather x2, waiting for transfers between devices, local(): gathered.append(lax.all_gather(block, axes, axis=0, tiled=False))  99.7 us
    pallas_call x2, Pallas kernels, pair_grads(): pl.pallas_call(functools.partial(pair_kernel, softmax_scale), grid_spec=p...  87.7 us
    all_gather x1, waiting for transfers between devices, local(): lax.all_gather(dequantize(cache_codes, cache_exponents, rank)[0], axes, a...  62.5 us
    all_gather x1, waiting for transfers between devices, local(): lax.all_gather(grad_keys.reshape(pages, page, full), axes, axis=0, tiled=...  60.6 us
    psum x1, waiting for transfers between devices, local(): weight_parts.append(lax.psum(mine[0], 'rep').astype(jnp.float32))  37.3 us
  transfers between devices with their start and end apart: 7, of which 7 were waited for; matrix products, arithmetic and copies ran while one was open for 3% of the time, Pallas kernels for 7%

profile of v1, /device:TPU:0, one launch (start us, length us, event | category | flops | bytes accessed | tf_op | source)
XLA Modules:
  0.0 609.7 jit_solution(2725565964018087173)
XLA Ops:
  7.2 0.0 copy-start
  7.2 0.0 all-gather.12.cloned.1.call-start
  7.2 0.8 exponential_bitcast_fusion
  8.0 0.9 slice.93
  8.9 0.2 copy.26
  9.1 0.4 broadcast_in_dim.22
  9.5 0.3 broadcast_in_dim.23
  9.8 1.1 multiply_convert_fusion
  10.9 0.8 pad_maximum_fusion.4
  11.7 0.0 all-gather.12.cloned.1.call-update
  11.7 0.0 all-gather.14.cloned.1.call-start
  11.8 1.4 slice_bitcast_fusion.9
  13.1 0.9 pad_maximum_fusion.3
  14.0 0.0 all-gather.14.cloned.1.call-update
  14.0 0.0 all-gather.10.cloned.1.call-start
  14.1 0.9 pad_maximum_fusion.2
  14.9 0.0 all-gather.10.cloned.1.call-update
  14.9 0.0 reduce-scatter.5.cloned.1.call-start
  15.0 0.1 copy.28
  15.1 0.1 reshape_squeeze.5
  15.2 0.1 dynamic-slice_bitcast_fusion.offset_ref
  15.3 0.1 compare_select_fusion.2
  15.4 62.5 %all-gather.12.cloned.1.call-done = bf16[1,320,16,576]{3,2,0,1:T(8,128)(2,1)} async-done(((bf16[1,20,16,576]{3,2,0,1:T(8,128)(2,1)}), bf16[1,320,16,576]{3,2,0,1:T(8,128)(2,1)}) %all-gather.12.cloned.1.call-update) | async-done | bytes 5898256 | tf_op jit(solution)/shard_map/all_gather | solution.py:159
  78.0 3.5 gather_fusion
  81.5 0.2 copy.30.lat_t_ref
  81.7 0.1 maximum_convert_fusion.rope_ref
  81.8 72.3 %all-gather.14.cloned.1.call-done = bf16[8192,512]{1,0:T(8,128)(2,1)} async-done(((bf16[512,512]{1,0:T(8,128)(2,1)}), bf16[8192,512]{1,0:T(8,128)(2,1)}) %all-gather.14.cloned.1.call-update) | async-done | bytes 8388624 | tf_op jit(solution)/shard_map/all_gather | solution.py:165
  154.2 0.1 broadcast_in_dim.25.base_lat_ref
  154.3 0.0 copy-start.2
  154.3 2.8 copy-done.2
  157.1 2.2 copy-done.4
  159.2 43.8 %pair_grads_0.1 = (bf16[4,64,12288]{2,1,0:T(8,128)(2,1)}, bf16[16,512,512]{2,1,0:T(8,128)(2,1)}, f32[320,512]{1,0:T(8,128)S(1)}, f32[320,128]{1,0:T(8,128)S(1)}) custom-call(s32[4]{0:T(128)S(1)} %dynamic-slice_bitcast_fusion.offset_ref, bf16[4,64,12288]{2,1,0:T(8,128)(2,1)S(1)} %bitcast.52, bf16[4,64,8192]{2,1,0:T(8,128)(2,1)S(1)} %bitcast.55, ...), custom_call_target="tpu_custom_call" | custom-call | flops 10234101760 | bytes 25165824 | tf_op jit(solution)/shard_map/pair_grads_0/pallas_call | solution.py:106
  203.0 27.3 %all-gather.10.cloned.1.call-done = bf16[8192,512]{1,0:T(8,128)(2,1)} async-done(((bf16[512,512]{1,0:T(8,128)(2,1)}), bf16[8192,512]{1,0:T(8,128)(2,1)}) %all-gather.10.cloned.1.call-update) | async-done | bytes 8388624 | tf_op jit(solution)/shard_map/all_gather | solution.py:165
  230.4 2.8 copy-done.3
  233.2 2.2 copy-done.5
  235.3 43.9 %pair_grads_1.1 = (bf16[4,64,12288]{2,1,0:T(8,128)(2,1)}, bf16[16,512,512]{2,1,0:T(8,128)(2,1)}, f32[320,512]{1,0:T(8,128)S(1)}, f32[320,128]{1,0:T(8,128)S(1)}) custom-call(s32[4]{0:T(128)S(1)} %dynamic-slice_bitcast_fusion.offset_ref, bf16[4,64,12288]{2,1,0:T(8,128)(2,1)S(1)} %bitcast.54, ...), custom_call_target="tpu_custom_call", output_to_operand_aliasing={{0}: (9, {})} | custom-call | flops 10234101760 | bytes 25165824 | tf_op jit(solution)/shard_map/pair_grads_1/pallas_call | solution.py:106
  279.2 0.0 reduce-scatter.5.cloned.1.call-update
  279.2 0.0 reduce-scatter.3.cloned.1.call-start
  279.3 0.5 reduce-scatter.3.cloned.1.call-update
  279.8 0.0 all-gather.8.cloned.1.call-start
  279.9 0.1 add_convert_fusion
  280.0 0.8 pad_maximum_fusion.5
  280.8 0.0 all-gather.8.cloned.1.call-update
  280.9 0.0 all-reduce.3.cloned.1.call-start
  280.9 101.4 %reduce-scatter.5.cloned.1.call-done = bf16[1,512,512]{2,1,0:T(8,128)(2,1)} async-done(((bf16[16,512,512]{2,1,0:T(8,128)(2,1)}), bf16[1,512,512]{2,1,0:T(8,128)(2,1)}) %reduce-scatter.5.cloned.1.call-update) | async-done | bytes 524304 | tf_op jit(solution)/shard_map/reduce_scatter | solution.py:187
  382.4 1.2 reshape.74
  383.5 0.9 copy.33
  384.4 106.4 %reduce-scatter.3.cloned.1.call-done = bf16[1,512,512]{2,1,0:T(8,128)(2,1)} async-done(((bf16[16,512,512]{2,1,0:T(8,128)(2,1)}), bf16[1,512,512]{2,1,0:T(8,128)(2,1)}) %reduce-scatter.3.cloned.1.call-update) | async-done | bytes 524304 | tf_op jit(solution)/shard_map/reduce_scatter | solution.py:187
  490.7 1.2 reshape.72
  491.9 0.9 copy.32
  492.8 0.0 all-reduce.3.cloned.1.call-update
  492.8 0.1 reshape_squeeze.6
  493.0 2.9 scatter_custom_fusion
  495.9 0.1 compare_select_fusion.1
  496.0 60.6 %all-gather.8.cloned.1.call-done = bf16[320,16,576]{2,1,0:T(8,128)(2,1)} async-done(((bf16[20,16,576]{2,1,0:T(8,128)(2,1)}), bf16[320,16,576]{2,1,0:T(8,128)(2,1)}) %all-gather.8.cloned.1.call-update) | async-done | bytes 5898256 | tf_op jit(solution)/shard_map/all_gather | solution.py:193
  556.6 3.5 gather_fusion.1
  560.1 0.9 bitcast_convert_fusion
  561.1 37.3 %all-reduce.3.cloned.1.call-done = (bf16[512,4,128]{2,0,1:T(8,128)(2,1)}, bf16[512,4,128]{2,0,1:T(8,128)(2,1)}) async-done(((bf16[512,4,128]{2,0,1:T(8,128)(2,1)}, bf16[512,4,128]{2,0,1:T(8,128)(2,1)}), (bf16[512,4,128]{2,0,1:T(8,128)(2,1)}, bf16[512,4,128]{2,0,1:T(8,128)(2,1)})) %all-reduce.3.cloned.1.call-update) | async-done | bytes 1048592 | tf_op jit(solution)/shard_map/psum | solution.py:188
  598.4 1.1 reshape.75
  599.5 0.1 slice_bitcast_fusion.1
  599.6 1.1 reshape.73
  600.7 0.1 slice_bitcast_fusion.3
  600.8 1.0 pad_maximum_fusion.1
  601.8 1.0 pad_maximum_fusion
  (16 shorter events, 0.2 us)
Async XLA Ops:
  7.2 8.1 %copy-start = (s32[1,64]{1,0:T(1,128)S(1)}, s32[1,64]{1,0:T(1,128)}, u32[]{:S(2)}) copy-start(s32[1,64]{1,0:T(1,128)} %param.13) | copy-start | bytes 772
  7.2 7.8 %copy-start.6 = (s32[1,64,5]{1,0,2:T(1,128)S(1)}, s32[1,64,5]{1,0,2:T(1,128)}, u32[]{:S(2)}) copy-start(s32[1,64,5]{1,0,2:T(1,128)} %param.12) | copy-start | bytes 3844
  7.2 70.8 %all-gather.12.cloned.1.call-start = ((), (), s32[]{:S(2)}) async-start(), calls=%async_computation.6 | async-start | bytes 6963200 | tf_op jit(solution)/shard_map/all_gather | solution.py:159
  11.7 142.5 %all-gather.14.cloned.1.call-start = ((), (), s32[]{:S(2)}) async-start(), calls=%async_computation.7 | async-start | bytes 8912896 | tf_op jit(solution)/shard_map/all_gather | solution.py:165
  14.0 216.4 %all-gather.10.cloned.1.call-start = ((), (), s32[]{:S(2)}) async-start(), calls=%async_computation.5 | async-start | bytes 8912896 | tf_op jit(solution)/shard_map/all_gather | solution.py:165
  14.9 367.4 %reduce-scatter.5.cloned.1.call-start = ((), (), s32[]{:S(2)}) async-start(), calls=%async_computation.4 | async-start | bytes 8912896 | tf_op jit(solution)/shard_map/reduce_scatter | solution.py:187
  154.3 2.8 copy-start.2
  157.1 2.2 copy-start.4
  230.4 2.8 copy-start.3
  233.2 2.2 copy-start.5
  279.2 211.5 %reduce-scatter.3.cloned.1.call-start = ((), (), s32[]{:S(2)}) async-start(), calls=%async_computation.3 | async-start | bytes 8912896 | tf_op jit(solution)/shard_map/reduce_scatter | solution.py:187
  279.8 276.8 %all-gather.8.cloned.1.call-start = ((), (), s32[]{:S(2)}) async-start(), calls=%async_computation.2 | async-start | bytes 6963200 | tf_op jit(solution)/shard_map/all_gather | solution.py:193
  280.9 317.5 %all-reduce.3.cloned.1.call-start = ((), (), s32[]{:S(2)}) async-start(), calls=%async_computation.8 | async-start | bytes 2097152 | tf_op jit(solution)/shard_map/psum | solution.py:188
  556.6 46.2 %copy-start.1 = (s32[1,64]{1,0:T(1,128)S(1)}, s32[1,64]{1,0:T(1,128)}, u32[]{:S(2)}) copy-start(s32[1,64]{1,0:T(1,128)} %param.13) | copy-start | bytes 772
Sparse Core Ops, SparseCore 0:
  11.8 66.0 all-gather.11
  80.7 73.4 all-gather.13
  156.9 73.4 all-gather.9
  279.4 102.9 reduce-scatter.4
  386.3 104.4 reduce-scatter.2
  493.4 63.1 all-gather.7
  559.6 38.7 all-reduce.2

commit v2 on v1

v2 whole, which is shorter than its diff:
```python
import functools

import jax
import jax.numpy as jnp
from jax import lax
from jax.experimental import pallas as pl
from jax.experimental.pallas import tpu as pltpu
from jax.sharding import PartitionSpec as P

LANES = 128
NT = (((1,), (1,)), ((), ()))
TN = (((0,), (0,)), ((), ()))


def dequantize(stored, exponents, rank):
    block_size = rank // exponents.shape[-1]
    factor = jnp.repeat(jnp.exp2(exponents.astype(jnp.float32)), block_size, axis=-1)
    latent = (stored[..., :rank].astype(jnp.float32) * factor).astype(jnp.bfloat16)
    return jnp.concatenate([latent, stored[..., rank:]], axis=-1)


def matmul(a, b, dims=None):
    if dims is None:
        return jnp.dot(a, b, preferred_element_type=jnp.float32)
    return lax.dot_general(a, b, dims, preferred_element_type=jnp.float32)


def pair_kernel(
    softmax_scale, offset_ref, q_ref, g_ref, w_ref, lat_ref, lat_t_ref, rope_ref,
    dq_ref, dw_ref, dlat_ref, drope_ref, kv_scratch, grad_scratch,
):
    seqs, rows, _ = q_ref.shape
    pairs = w_ref.shape[0]
    width = q_ref.shape[2] // pairs
    v_width = g_ref.shape[2] // pairs
    keys = lat_ref.shape[0] // seqs
    half = LANES // 2

    @pl.when(pl.program_id(0) == 0)
    def _():
        dlat_ref[...] = jnp.zeros_like(dlat_ref)
        drope_ref[...] = jnp.zeros_like(drope_ref)

    low = lax.broadcasted_iota(jnp.int32, (lat_ref.shape[0], LANES), 1) < half
    lane_q = lax.broadcasted_iota(jnp.int32, (rows, width), 1) < width // 2
    key_at = lax.broadcasted_iota(jnp.int32, (keys, 2 * rows), 0)
    lane = lax.broadcasted_iota(jnp.int32, (keys, 2 * rows), 1)
    query_at = jnp.where(lane < rows, lane, lane - rows)
    zero_g = jnp.zeros((rows, LANES), jnp.bfloat16)
    zero_q = jnp.zeros((rows, width), jnp.bfloat16)
    low_s = low[:keys]

    def up(p):
        kv = matmul(lat_ref[...], w_ref[p])
        rope = rope_ref[...]
        turned = pltpu.roll(kv[:, LANES : 2 * LANES], half, 1)
        kv_scratch[p, :, :LANES] = kv[:, :LANES].astype(jnp.bfloat16)
        kv_scratch[p, :, LANES : 2 * LANES] = jnp.where(low, rope, turned).astype(jnp.bfloat16)
        kv_scratch[p, :, 2 * LANES : width] = jnp.where(low, turned, rope).astype(jnp.bfloat16)
        kv_scratch[p, :, width:] = kv[:, 2 * LANES :].astype(jnp.bfloat16)

    def attend(p, s):
        span = slice(s * keys, (s + 1) * keys)
        q = q_ref[s, :, p * width : (p + 1) * width]
        q_two = jnp.concatenate([jnp.where(lane_q, q, zero_q), jnp.where(lane_q, zero_q, q)], axis=0)
        g = g_ref[s, :, p * v_width : (p + 1) * v_width]
        g_two = jnp.concatenate(
            [
                jnp.concatenate([g[:, :LANES], zero_g], axis=1),
                jnp.concatenate([zero_g, g[:, LANES:]], axis=1),
            ],
            axis=0,
        )
        k = kv_scratch[p, span, :width]
        v = kv_scratch[p, span, width:]
        scores = matmul(k, q_two, NT) * softmax_scale
        grad_attention = matmul(v, g_two, NT)
        visible = key_at <= query_at + offset_ref[s]
        scores = jnp.where(visible, scores, -jnp.inf)
        exp_scores = jnp.exp(scores - jnp.max(scores, axis=0, keepdims=True))
        attention = exp_scores / jnp.sum(exp_scores, axis=0, keepdims=True)
        attention_low = attention.astype(jnp.bfloat16)
        row_delta = jnp.sum(attention_low.astype(jnp.float32) * grad_attention, axis=0, keepdims=True)
        grad_scores = (attention * (grad_attention - row_delta) * softmax_scale).astype(jnp.bfloat16)
        dq = matmul(grad_scores, k, TN)
        dk = matmul(grad_scores, q_two)
        dv = matmul(attention_low, g_two)
        dq_ref[s, :, p * width : (p + 1) * width] = jnp.where(lane_q, dq[:rows], dq[rows:]).astype(jnp.bfloat16)
        first, middle, last = dk[:, :LANES], dk[:, LANES : 2 * LANES], dk[:, 2 * LANES :]
        drope_ref[span, :] += jnp.where(low_s, middle, last)
        second = pltpu.roll(jnp.where(low_s, last, middle), half, 1)
        grad_scratch[p, span, :LANES] = first.astype(jnp.bfloat16)
        grad_scratch[p, span, LANES : 2 * LANES] = second.astype(jnp.bfloat16)
        grad_scratch[p, span, 2 * LANES :] = dv.astype(jnp.bfloat16)

    def down(p):
        grads = grad_scratch[p]
        dlat_ref[...] += matmul(grads, w_ref[p], NT)
        dw_ref[p] = matmul(lat_t_ref[...], grads).astype(jnp.bfloat16)

    for step in range(pairs + 2):
        if step < pairs:
            up(step)
        if 0 <= step - 1 < pairs:
            for s in range(seqs):
                attend(step - 1, s)
        if step >= 2:
            down(step - 2)


def pair_grads(offsets, queries, grads, weights, lat, lat_t, rope2):
    pairs, rank, columns = weights.shape
    seqs, rows, _ = queries.shape
    key_rows = lat.shape[0]
    block = next(n for n in (4, 2, 1) if pairs % n == 0)
    width = queries.shape[2] // (pairs)
    v_width = grads.shape[2] // (pairs)
    softmax_scale = (width // 2) ** (-0.5)
    whole = lambda i, off: (0, 0)
    rows_of = lambda i, off: (0, 0, i)
    return pl.pallas_call(
        functools.partial(pair_kernel, softmax_scale),
        grid_spec=pltpu.PrefetchScalarGridSpec(
            num_scalar_prefetch=1,
            grid=(pairs // block,),
            in_specs=[
                pl.BlockSpec((seqs, rows, block * width), rows_of),
                pl.BlockSpec((seqs, rows, block * v_width), rows_of),
                pl.BlockSpec((block, rank, columns), lambda i, off: (i, 0, 0)),
                pl.BlockSpec((key_rows, rank), whole),
                pl.BlockSpec((rank, key_rows), whole),
                pl.BlockSpec((key_rows, LANES), whole),
            ],
            out_specs=[
                pl.BlockSpec((seqs, rows, block * width), rows_of),
                pl.BlockSpec((block, rank, columns), lambda i, off: (i, 0, 0)),
                pl.BlockSpec((key_rows, rank), whole),
                pl.BlockSpec((key_rows, LANES), whole),
            ],
            scratch_shapes=[
                pltpu.VMEM((block, key_rows, width + v_width), jnp.bfloat16),
                pltpu.VMEM((block, key_rows, columns), jnp.bfloat16),
            ],
        ),
        out_shape=[
            jax.ShapeDtypeStruct(queries.shape, jnp.bfloat16),
            jax.ShapeDtypeStruct(weights.shape, jnp.bfloat16),
            jax.ShapeDtypeStruct((key_rows, rank), jnp.float32),
            jax.ShapeDtypeStruct((key_rows, LANES), jnp.float32),
        ],
        compiler_params=pltpu.CompilerParams(vmem_limit_bytes=40 * 2**20),
        cost_estimate=pl.CostEstimate(
            flops=pairs * 2 * (3 * key_rows * rank * columns + key_rows * 2 * rows * (3 * width + 2 * v_width)),
            bytes_accessed=pairs * (2 * seqs * rows * (2 * width + v_width) + 4 * rank * columns),
            transcendentals=pairs * key_rows * 2 * rows,
        ),
        name="pair_grads",
    )(offsets, queries, grads, weights, lat, lat_t, rope2)


CORES = 2
MESH = pl.DeviceIdType.MESH


def place():
    column = lax.axis_index("sb")
    return lax.axis_index("sa"), column // CORES, column % CORES, lax.axis_index("rep")


def device(z, x, c, r):
    return {"sa": z, "sb": x * CORES + c, "rep": r}


def gather_kernel(
    depth, columns, reps, w_ref, p_ref, w_out, p_out,
    local_sem, w_send, w_recv, p_send, p_recv,
):
    z, x, c, r = place()
    rows = w_ref.shape[1] // reps

    def owner_of(z_at, x_at, c_at):
        return (z_at * columns + x_at) * CORES + c_at

    me = owner_of(z, x, c)
    other = 1 - c
    barrier = pltpu.get_barrier_semaphore()
    greeted = [
        (z + 1 < depth, (z + 1, x, c, r)),
        (z > 0, (z - 1, x, c, r)),
        (x + 1 < columns, (z, x + 1, c, r)),
        (x > 0, (z, x - 1, c, r)),
        (None, (z, x, other, r)),
    ] + [(None, (z, x, c, lax.rem(r + k, reps))) for k in range(1, reps)]
    for valid, peer in greeted:
        def greet(peer=peer):
            pl.semaphore_signal(barrier, inc=1, device_id=device(*peer), device_id_type=MESH)
        if valid is None:
            greet()
        else:
            pl.when(valid)(greet)
    pl.semaphore_wait(barrier, sum(1 if valid is None else valid.astype(jnp.int32) for valid, _ in greeted))

    def weights_of(ref, part):
        if part is None:
            return ref
        return ref.at[:, pl.ds(part * rows, rows), :]

    def weight_copy(owner, part, kind, peer):
        source = w_ref if owner is me else w_out.at[owner]
        slot = 0 if part is None else part
        return pltpu.make_async_remote_copy(
            src_ref=weights_of(source, part),
            dst_ref=weights_of(w_out.at[owner], part),
            send_sem=w_send.at[kind, owner, slot],
            recv_sem=w_recv.at[owner, slot],
            device_id=device(*peer),
            device_id_type=MESH,
        )

    def page_copy(owner, kind, peer):
        return pltpu.make_async_remote_copy(
            src_ref=p_ref if owner is me else p_out.at[owner],
            dst_ref=p_out.at[owner],
            send_sem=p_send.at[kind, owner],
            recv_sem=p_recv.at[owner],
            device_id=device(*peer),
            device_id_type=MESH,
        )

    def receive_weights(owner, part):
        weight_copy(owner, part, 0, (z, x, other, r)).wait_recv()

    def receive_pages(owner):
        page_copy(owner, 0, (z, x, other, r)).wait_recv()

    def walk(act, receive):
        def send_weights(owner, part, kind, peer):
            act(weight_copy(owner, part, kind, peer))

        def send_pages(owner, kind, peer):
            act(page_copy(owner, kind, peer))

        def along_x(owner, up, down):
            def one_way(kind, to):
                send_weights(owner, r, kind, (z, to, c, r))
                send_pages(owner, kind, (z, to, c, r))
            if up:
                pl.when(x + 1 < columns)(lambda: one_way(2, x + 1))
            if down:
                pl.when(x > 0)(lambda: one_way(3, x - 1))

        def along_z(owner, up, down):
            def one_way(kind, to):
                send_pages(owner, kind, (to, x, c, r))
                send_weights(owner, None, kind, (to, x, c, r))
            if up:
                pl.when(z + 1 < depth)(lambda: one_way(0, z + 1))
            if down:
                pl.when(z > 0)(lambda: one_way(1, z - 1))

        def to_core(owner, part):
            send_weights(owner, part, 4, (z, x, other, r))

        def page_to_core(owner):
            send_pages(owner, 4, (z, x, other, r))

        along_z(me, True, True)
        along_x(me, True, True)
        page_to_core(me)
        to_core(me, None)

        def from_x(x_at, z_at, up):
            owner = owner_of(z_at, x_at, c)
            if receive:
                receive_pages(owner)
                receive_weights(owner, r)
            along_x(owner, up, not up)
            page_to_core(owner)
            for k in range(1, reps):
                send_weights(owner, r, 4 + k, (z, x, c, lax.rem(r + k, reps)))
            to_core(owner, r)

        def rest(x_at, z_at):
            owner = owner_of(z_at, x_at, c)
            for k in range(1, reps):
                part = lax.rem(r + k, reps)
                if receive:
                    receive_weights(owner, part)
                to_core(owner, part)

        def from_z(z_at, up):
            owner = owner_of(z_at, x, c)
            if receive:
                receive_pages(owner)
                receive_weights(owner, None)
            along_z(owner, up, not up)
            along_x(owner, True, True)
            page_to_core(owner)
            to_core(owner, None)

        def at_z(step, visit):
            if step == 0:
                visit(z, None)
                return
            pl.when(z - step >= 0)(lambda: visit(z - step, True))
            pl.when(z + step < depth)(lambda: visit(z + step, False))

        def at_x(visit):
            for far in range(1, columns):
                pl.when(x - far >= 0)(lambda: visit(x - far, True))
                pl.when(x + far < columns)(lambda: visit(x + far, False))

        for step in range(depth):
            if step > 0:
                at_z(step, from_z)
            at_x(lambda x_at, up: at_z(step, lambda z_at, _: from_x(x_at, z_at, up)))
            if step > 0:
                at_x(lambda x_at, up: at_z(step - 1, lambda z_at, _: rest(x_at, z_at)))
        at_x(lambda x_at, up: at_z(depth - 1, lambda z_at, _: rest(x_at, z_at)))

    own_copies = [
        pltpu.make_async_copy(w_ref, w_out.at[me], local_sem.at[0]),
        pltpu.make_async_copy(p_ref, p_out.at[me], local_sem.at[1]),
    ]
    for copy in own_copies:
        copy.start()
    walk(lambda copy: copy.start(), True)

    def from_core(x_at, parts):
        for z_at in range(depth):
            owner = owner_of(z_at, x_at, other)
            receive_pages(owner)
            for part in parts:
                receive_weights(owner, part)

    from_core(x, [None])
    for far in range(1, columns):
        from_core(lax.rem(x + far, columns), list(range(reps)))
    walk(lambda copy: copy.wait_send(), False)
    for copy in own_copies:
        copy.wait()


def gather_all(weights, pages, depth, columns, reps):
    owners = depth * columns * CORES
    anywhere = pl.BlockSpec(memory_space=pl.ANY)
    kinds = 4 + reps
    return pl.pallas_call(
        functools.partial(gather_kernel, depth, columns, reps),
        in_specs=[anywhere] * 2,
        out_specs=[anywhere] * 2,
        out_shape=[
            jax.ShapeDtypeStruct((owners,) + weights.shape, weights.dtype),
            jax.ShapeDtypeStruct((owners,) + pages.shape, pages.dtype),
        ],
        scratch_shapes=[
            pltpu.SemaphoreType.DMA((2,)),
            pltpu.SemaphoreType.DMA((kinds, owners, reps)),
            pltpu.SemaphoreType.DMA((owners, reps)),
            pltpu.SemaphoreType.DMA((kinds, owners)),
            pltpu.SemaphoreType.DMA((owners,)),
        ],
        compiler_params=pltpu.CompilerParams(collective_id=0, has_side_effects=True),
        cost_estimate=pl.CostEstimate(flops=0, bytes_accessed=2 * owners * weights.size * 2, transcendentals=0),
        name="gather_all",
    )(weights, pages)


def reduce_kernel(
    depth, columns, reps, d_ref, out_ref,
    own, core_in, y_low_in, x_high_in, x_low_in, y_high_in, z_in, final,
    load_sem, core_sem, y_low_sem, x_high_sem, x_low_sem, y_high_sem, z_sem, final_sem,
):
    z, x, c, r = place()
    other = 1 - c
    chunks, rank, _ = out_ref.shape
    half = rank // 2
    share = half // reps

    def turn(value, by, size):
        return lax.rem(value + by, size)

    peers = [(z, x, other, r)]
    peers += [(z, turn(x, k, columns), c, r) for k in range(1, columns)]
    peers += [(z, x, c, turn(r, k, reps)) for k in range(1, reps)]
    peers += [(turn(z, k, depth), x, c, r) for k in range(1, depth)]
    barrier = pltpu.get_barrier_semaphore()
    for peer in peers:
        pl.semaphore_signal(barrier, inc=1, device_id=device(*peer), device_id_type=MESH)
    pl.semaphore_wait(barrier, len(peers))

    def send(source, target, sems, at, peer):
        copy = pltpu.make_async_remote_copy(
            src_ref=source,
            dst_ref=target,
            send_sem=sems.at[(0,) + at],
            recv_sem=sems.at[(1,) + at],
            device_id=device(*peer),
            device_id_type=MESH,
        )
        copy.start()
        return copy

    def low(part):
        return pl.ds(pl.multiple_of(part * share, share), share)

    def high(part):
        return pl.ds(pl.multiple_of(half + part * share, share), share)

    groups = 2 if chunks % 2 == 0 else 1
    size = chunks // groups

    def of_group(g):
        return pl.ds(g * size, size)

    def each(g, visit):
        def step(i, carry):
            visit(i // size, g * size + i % size)
            return carry
        lax.fori_loop(0, depth * size, step, 0)

    def total(*terms):
        value = terms[0].astype(jnp.float32)
        for term in terms[1:]:
            value = value + term.astype(jnp.float32)
        return value.astype(jnp.bfloat16)

    order = [turn(x, k, columns) for k in range(1, columns)] + [x]
    loads, crossed = {}, {}
    for g in range(groups):
        for i, x_at in enumerate(order):
            crossed[g, i] = send(
                d_ref.at[:, x_at, other, of_group(g)], core_in.at[x_at, :, of_group(g)], core_sem, (g, i),
                (z, x, other, r),
            )
            loads[g, i] = pltpu.make_async_copy(
                d_ref.at[:, x_at, c, of_group(g)], own.at[x_at, :, of_group(g)], load_sem.at[g, i]
            )
            loads[g, i].start()
    y_low, x_high, x_low, y_high, along_z, last = {}, {}, {}, {}, {}, {}

    def add_cores(g, i):
        x_at = order[i]
        loads[g, i].wait()
        crossed[g, i].wait_recv()

        def add(zi, ci):
            for rows in (slice(0, half), slice(half, rank)):
                own[x_at, zi, ci, rows, :] = total(own[x_at, zi, ci, rows, :], core_in[x_at, zi, ci, rows, :])

        each(g, add)

    def send_first(g, i):
        x_at = order[i]
        if i < columns - 1:
            x_high[g, i] = send(
                own.at[x_at, :, of_group(g), pl.ds(half, half), :], x_high_in.at[i, :, of_group(g)],
                x_high_sem, (g, i), (z, x_at, c, r),
            )
        for k in range(1, reps):
            part = turn(r, k, reps)
            y_low[g, k, i] = send(
                own.at[x_at, :, of_group(g), low(part), :], y_low_in.at[k - 1, i, :, of_group(g)],
                y_low_sem, (g, k - 1, i), (z, x, c, part),
            )

    def wait_first(g):
        for i in range(columns):
            for k in range(1, reps):
                y_low[g, k, i].wait_recv()
        for i in range(columns - 1):
            x_high[g, i].wait_recv()

    def send_second(g):
        for i, x_at in enumerate(order):
            def add_low(zi, ci):
                terms = [own[x_at, zi, ci, low(r), :]] + [y_low_in[k, i, zi, ci] for k in range(reps - 1)]
                own[x_at, zi, ci, low(r), :] = total(*terms)

            each(g, add_low)
            if i < columns - 1:
                x_low[g, i] = send(
                    own.at[x_at, :, of_group(g), low(r), :], x_low_in.at[i, :, of_group(g)],
                    x_low_sem, (g, i), (z, x_at, c, r),
                )

        def add_high(zi, ci):
            terms = [own[x, zi, ci, half:, :]] + [x_high_in[k, zi, ci] for k in range(columns - 1)]
            own[x, zi, ci, half:, :] = total(*terms)

        each(g, add_high)
        for k in range(1, reps):
            part = turn(r, k, reps)
            y_high[g, k] = send(
                own.at[x, :, of_group(g), high(part), :], y_high_in.at[k - 1, :, of_group(g)],
                y_high_sem, (g, k - 1), (z, x, c, part),
            )

    def send_along_z(g):
        for i in range(columns - 1):
            x_low[g, i].wait_recv()

        def add_low(zi, ci):
            terms = [own[x, zi, ci, low(r), :]] + [x_low_in[k, zi, ci] for k in range(columns - 1)]
            own[x, zi, ci, low(r), :] = total(*terms)

        each(g, add_low)
        for k in range(1, reps):
            y_high[g, k].wait_recv()

        def add_high(zi, ci):
            terms = [own[x, zi, ci, high(r), :]] + [y_high_in[k, zi, ci] for k in range(reps - 1)]
            own[x, zi, ci, high(r), :] = total(*terms)

        each(g, add_high)
        for s, rows_of in enumerate((low, high)):
            for k in range(1, depth):
                z_at = turn(z, k, depth)
                along_z[g, s, k] = send(
                    own.at[x, z_at, of_group(g), rows_of(r), :], z_in.at[k - 1, s, of_group(g)],
                    z_sem, (g, k - 1, s), (z_at, x, c, r),
                )

    def send_last(g):
        for s, rows_of in enumerate((low, high)):
            for k in range(1, depth):
                along_z[g, s, k].wait_recv()
            for ci in range(g * size, (g + 1) * size):
                terms = [own[x, z, ci, rows_of(r), :]] + [z_in[k, s, ci] for k in range(depth - 1)]
                final[ci, rows_of(r), :] = total(*terms)
            for k in range(1, reps):
                mine = final.at[of_group(g), rows_of(r), :]
                last[g, s, k] = send(mine, mine, final_sem, (g, k - 1, s), (z, x, c, turn(r, k, reps)))

    for i in range(columns):
        add_cores(0, i)
        send_first(0, i)
    for g in range(1, groups):
        for i in range(columns):
            add_cores(g, i)
    wait_first(0)
    for g in range(1, groups):
        for i in range(columns):
            send_first(g, i)
    send_second(0)
    send_along_z(0)
    for g in range(1, groups):
        wait_first(g)
        send_second(g)
    send_last(0)
    for g in range(1, groups):
        send_along_z(g)
        send_last(g)
    for copy in last.values():
        copy.wait_recv()
    for ci in range(chunks):
        out_ref[ci] = final[ci].astype(jnp.float32)
    for copies in (crossed, y_low, x_high, x_low, y_high, along_z, last):
        for copy in copies.values():
            copy.wait_send()


def reduce_all(partial, depth, columns, reps):
    chunks, rank, width = partial.shape[3:]
    half = rank // 2
    share = half // reps
    dma = pltpu.SemaphoreType.DMA
    kept = lambda *shape: pltpu.VMEM(shape, jnp.bfloat16)
    lone = lambda size: max(size, 1)
    return pl.pallas_call(
        functools.partial(reduce_kernel, depth, columns, reps),
        in_specs=[pl.BlockSpec(memory_space=pl.ANY)],
        out_specs=pl.BlockSpec(memory_space=pltpu.VMEM),
        out_shape=jax.ShapeDtypeStruct((chunks, rank, width), jnp.float32),
        scratch_shapes=[
            kept(columns, depth, chunks, rank, width),
            kept(columns, depth, chunks, rank, width),
            kept(lone(reps - 1), columns, depth, chunks, share, width),
            kept(lone(columns - 1), depth, chunks, half, width),
            kept(lone(columns - 1), depth, chunks, share, width),
            kept(lone(reps - 1), depth, chunks, share, width),
            kept(lone(depth - 1), 2, chunks, share, width),
            kept(chunks, rank, width),
            dma((2, columns)),
            dma((2, 2, columns)),
            dma((2, 2, lone(reps - 1), columns)),
            dma((2, 2, lone(columns - 1))),
            dma((2, 2, lone(columns - 1))),
            dma((2, 2, lone(reps - 1))),
            dma((2, 2, lone(depth - 1), 2)),
            dma((2, 2, lone(reps - 1), 2)),
        ],
        compiler_params=pltpu.CompilerParams(
            collective_id=1, has_side_effects=True, vmem_limit_bytes=48 * 2**20
        ),
        cost_estimate=pl.CostEstimate(flops=partial.size, bytes_accessed=2 * partial.size, transcendentals=0),
        name="reduce_all",
    )(partial)


def local(depth, columns, reps, queries, grad_out, cache_codes, cache_exponents, page_table, offsets, key_up, value_up):
    axes = ("sa", "sb")
    heads, rank, nope = key_up.shape
    _, seqs, rows, _ = queries.shape
    pages, page, full = cache_codes.shape[1:]
    rope_width = full - rank
    me = lax.axis_index(axes)
    chunks = heads // 2

    def side_by_side(heads_of):
        paired = heads_of.reshape(chunks, 2, rank, nope)
        return jnp.swapaxes(paired, 1, 2).reshape(chunks, rank, 2 * nope)

    own_weights = jnp.concatenate([side_by_side(key_up), side_by_side(value_up)], axis=2)
    own_pages = dequantize(cache_codes, cache_exponents, rank)[0].reshape(pages * page, full)
    weights, pool = gather_all(own_weights, own_pages, depth, columns, reps)
    owners = weights.shape[0]
    weights = weights.reshape((owners * chunks,) + weights.shape[2:])
    pool = pool.reshape(owners * pages, page, full)

    table = page_table[0].reshape(-1)
    own = lax.dynamic_slice_in_dim(table, me * pages, pages)
    inverse = jnp.zeros_like(table).at[table].set(jnp.arange(table.shape[0], dtype=table.dtype))
    own_inverse = lax.dynamic_slice_in_dim(inverse, me * pages, pages)
    my_offsets = lax.dynamic_slice_in_dim(offsets[0], me * seqs, seqs)

    keys = pool[own].reshape(pages * page, full)
    lat = keys[:, :rank]
    lat_t = lat.T
    rope = keys[:, rank:].astype(jnp.float32)
    rope2 = jnp.concatenate([rope, rope], axis=1)
    grad_queries, dw, grad_lat, grad_rope = pair_grads(
        my_offsets, queries[0], grad_out[0], weights, lat, lat_t, rope2
    )
    grad_keys = jnp.concatenate(
        [grad_lat, grad_rope[:, :rope_width] + grad_rope[:, rope_width:]], axis=1
    ).astype(jnp.bfloat16)
    all_pages = lax.all_gather(grad_keys.reshape(pages, page, full), axes, axis=0, tiled=True)
    grad_cache = all_pages[own_inverse].astype(jnp.float32)[None]
    mine = reduce_all(dw.reshape((depth, columns, CORES, chunks) + dw.shape[1:]), depth, columns, reps)
    split = mine.reshape(chunks, rank, 4, nope)
    grad_key_up = jnp.swapaxes(split[:, :, :2], 1, 2).reshape(heads, rank, nope)
    grad_value_up = jnp.swapaxes(split[:, :, 2:], 1, 2).reshape(heads, rank, nope)
    return (grad_queries[None], grad_cache, grad_key_up, grad_value_up)


def solution(mesh):
    in_specs = (
        P("rep", ("sa", "sb"), None, None),
        P("rep", ("sa", "sb"), None, None),
        P("rep", ("sa", "sb"), None, None),
        P("rep", ("sa", "sb"), None, None),
        P("rep", None, None),
        P("rep", None),
        P(("sa", "sb"), None, None),
        P(("sa", "sb"), None, None),
    )
    out_specs = (
        P("rep", ("sa", "sb"), None, None),
        P("rep", ("sa", "sb"), None, None),
        P(("sa", "sb"), None, None),
        P(("sa", "sb"), None, None),
    )
    sizes = (mesh.shape["sa"], mesh.shape["sb"] // CORES, mesh.shape["rep"])
    return jax.shard_map(functools.partial(local, *sizes), mesh=mesh, in_specs=in_specs, out_specs=out_specs, check_vma=False)
```

time: 610 us -> 405 us (0.66)
  waiting for transfers between devices: 469 us -> 0.02 us
  Pallas kernels: 87.7 us -> 358 us
    pallas_call x0 -> x2, Pallas kernels: none -> 282 us  [the longest x1 145 us: gather_all(): pl.pallas_call(functools.partial(gather_kernel, depth, columns, reps), in...]
    reduce_scatter x2 -> x0, waiting for transfers between devices: 208 us -> none  [local(): mine = lax.psum_scatter(dw, axes, scatter_dimension=0, tiled=True)]
    all_gather x3 -> x0, waiting for transfers between devices: 162 us -> none  [the longest x2 99.7 us: local(): gathered.append(lax.all_gather(block, axes, axis=0, tiled=False))]
    all_gather x1, waiting for transfers between devices: 60.6 us -> 0.01 us  [local(): lax.all_gather(grad_keys.reshape(pages, page, full), axes, axis=0, tiled=...]
    psum x1 -> x0, waiting for transfers between devices: 37.3 us -> none  [local(): weight_parts.append(lax.psum(mine[0], 'rep').astype(jnp.float32))]
    pallas_call x2 -> x1, Pallas kernels: 87.7 us -> 75.8 us  [pair_grads(): pl.pallas_call(functools.partial(pair_kernel, softmax_scale), grid_spec=p...]
  transfers between devices with their start and end apart: 7 -> 1, of which waited for: 7 -> 0; matrix products, arithmetic and copies ran while one was open for 3% -> 3% of each run, Pallas kernels for 7% -> 34%
where the time goes in v2:
time: 405 us
  Pallas kernels  358 us (88%)
  local copies, waits for them, and re-layouts  27.1 us (7%)
  between operations  14.2 us (4%)
  other arithmetic  5.88 us (1%)
    pallas_call x1, Pallas kernels, gather_all(): pl.pallas_call(functools.partial(gather_kernel, depth, columns, reps), in...  145 us
    pallas_call x1, Pallas kernels, reduce_all(): pl.pallas_call(functools.partial(reduce_kernel, depth, columns, reps), in...  137 us
    pallas_call x1, Pallas kernels, pair_grads(): pl.pallas_call(functools.partial(pair_kernel, softmax_scale), grid_spec=p...  75.8 us
  transfers between devices with their start and end apart: 1, of which 0 were waited for; matrix products, arithmetic and copies ran while one was open for 3% of the time, Pallas kernels for 34%

profile of v2, /device:TPU:0, one launch (start us, length us, event | category | flops | bytes accessed | tf_op | source)
XLA Modules:
  0.0 405.1 jit_solution(1483616012518355114)
XLA Ops:
  7.2 0.0 copy-start
  7.2 0.0 slice-start
  7.2 0.0 copy-start.4
  7.2 0.0 all-gather.2.cloned.1.call-start
  7.3 0.8 copy.29
  8.1 0.1 reshape_squeeze.9
  8.2 0.1 compare_select_fusion.2
  8.3 0.8 exponential_bitcast_fusion
  9.1 0.2 copy.28
  9.3 0.4 broadcast_in_dim.16
  9.7 0.3 broadcast_in_dim.17
  10.0 1.1 multiply_convert_fusion
  11.1 1.6 copy.37
  12.7 0.3 reshape.90
  13.0 0.0 copy-done.4
  13.0 0.5 copy.36
  13.6 0.3 reshape.92
  13.9 0.0 slice-done
  13.9 0.8 pad_maximum_fusion.1
  14.7 1.1 pad_maximum_fusion.w_ref
  15.8 144.7 %gather_all.1 = (bf16[16,2,512,512]{3,2,1,0:T(8,128)(2,1)}, bf16[16,320,576]{2,1,0:T(8,128)(2,1)}) custom-call(bf16[2,512,512]{2,1,0:T(8,128)(2,1)} %pad_maximum_fusion.w_ref, bf16[320,576]{1,0:T(8,128)(2,1)} %bitcast.39), custom_call_target="tpu_custom_call" | custom-call | bytes 33554432 | tf_op jit(solution)/shard_map/gather_all/pallas_call | solution.py:348
  160.5 3.5 gather_fusion
  164.0 0.1 maximum_convert_fusion.rope_ref
  164.1 0.2 copy.30.lat_t_ref
  164.3 0.0 copy-done
  164.3 0.1 dynamic-slice_bitcast_fusion.offset_ref
  164.4 0.0 copy-start.2
  164.4 2.8 copy-done.2
  167.2 0.0 copy-start.3
  167.2 2.2 copy-done.3
  169.4 75.8 %pair_grads.1 = (bf16[4,64,12288]{2,1,0:T(8,128)(2,1)}, bf16[32,512,512]{2,1,0:T(8,128)(2,1)}, f32[320,512]{1,0:T(8,128)S(1)}, f32[320,128]{1,0:T(8,128)S(1)}) custom-call(s32[4]{0:T(128)S(1)} %dynamic-slice_bitcast_fusion.offset_ref, bf16[4,64,12288]{2,1,0:T(8,128)(2,1)S(1)} %bitcast.34, bf16[4,64,8192]{2,1,0:T(8,128)(2,1)S(1)} %bitcast.35, ...), custom_call_target="tpu_custom_call" | custom-call | flops 20468203520 | bytes 50331648 | tf_op jit(solution)/shard_map/pair_grads/pallas_call | solution.py:121
  245.2 0.1 add_convert_fusion
  245.3 0.8 pad_maximum_fusion.2
  246.1 0.0 all-gather.2.cloned.1.call-update
  246.2 0.1 reshape_squeeze.10
  246.3 0.0 copy-start.1
  246.3 137.4 %reduce_all.1 = f32[2,512,512]{2,1,0:T(8,128)S(1)} custom-call(bf16[4,2,2,2,512,512]{5,4,3,2,1,0:T(8,128)(2,1)} %bitcast.36), custom_call_target="tpu_custom_call" | custom-call | flops 8388608 | bytes 16777216 | tf_op jit(solution)/shard_map/reduce_all/pallas_call | solution.py:570
  383.7 1.8 reshape.97
  385.5 3.2 slice_bitcast_fusion
  388.7 1.0 copy.33
  389.7 1.0 copy.32
  390.8 2.9 scatter_custom_fusion
  393.7 0.1 compare_select_fusion.1
  393.8 0.0 all-gather.2.cloned.1.call-done
  393.8 3.5 gather_fusion.1
  397.3 0.9 bitcast_convert_fusion
  398.2 0.0 copy-done.1
  (7 shorter events, 0.1 us)
Async XLA Ops:
  7.2 157.2 %copy-start = (s32[1,64]{1,0:T(1,128)S(1)}, s32[1,64]{1,0:T(1,128)}, u32[]{:S(2)}) copy-start(s32[1,64]{1,0:T(1,128)} %param.13) | copy-start | bytes 772
  7.2 6.7 %slice-start = ((bf16[1,20,16,576]{3,2,1,0:T(8,128)(2,1)}), bf16[1,20,16,64]{3,2,1,0:T(8,128)(2,1)S(1)}, s32[]{:S(2)}) async-start(bf16[1,20,16,576]{3,2,1,0:T(8,128)(2,1)} %param.10), calls=%async_computation.1 | async-start | bytes 163840 | tf_op jit(solution)/shard_map/slice | solution.py:19
  7.2 5.8 %copy-start.4 = (bf16[4,512,128]{2,1,0:T(8,128)(2,1)S(1)}, bf16[4,512,128]{2,1,0:T(8,128)(2,1)}, u32[]{:S(2)}) copy-start(bf16[4,512,128]{2,1,0:T(8,128)(2,1)} %param.15) | copy-start | bytes 1572868
  7.2 386.6 %all-gather.2.cloned.1.call-start = ((), (), s32[]{:S(2)}) async-start(), calls=%async_computation | async-start | bytes 6963200 | tf_op jit(solution)/shard_map/all_gather | solution.py:638
  164.4 2.8 copy-start.2
  167.2 2.2 copy-start.3
  246.3 151.9 %copy-start.1 = (s32[1,64]{1,0:T(1,128)S(1)}, s32[1,64]{1,0:T(1,128)}, u32[]{:S(2)}) copy-start(s32[1,64]{1,0:T(1,128)} %param.13) | copy-start | bytes 772
Sparse Core Ops, SparseCore 0:
  246.3 82.7 all-gather.1
